TPU v7x, 512 devices: a whole 4x8x8 slice. The times are simulated.
512 devices in a mesh: section: 32 (over x, y), tensor: 16 (over z, core).
Axes of the slice: x: 4, y: 8, z: 8, core: 2. Of those that a mesh axis runs over, the one named last changes fastest.
Arguments:
- frozen: bfloat16 [32, 14336, 2048], P('section', 'tensor'), may hold values from -1 to 1, as said below
- adapter_a: bfloat16 [32, 8, 14336], P('section', None, 'tensor'), may hold values from -0.119628906 to 0.119628906
- adapter_b: bfloat16 [32, 16, 2048], P('section'), may hold values from -0.22460938 to 0.22460938
- magnitude: float32 [32, 2048], P('section'), may hold values from 0.5 to 2
- hidden_fwd: bfloat16 [32, 128, 14336], P('section', None, 'tensor'), may hold values from -6 to 6
- carried: bfloat16 [32, 256, 2048], P('section', 'tensor'), may hold values from -6 to 6
- embedded: bfloat16 [256, 4096], P('tensor'), may hold values from -6 to 6
- hidden_bwd: bfloat16 [32, 128, 14336], P('section', None, 'tensor'), may hold values from -6 to 6
- returned: bfloat16 [32, 256, 2048], P('section', 'tensor'), may hold values from -1.5 to 1.5
- head_grad: bfloat16 [256, 4096], P('tensor'), may hold values from -1.5 to 1.5
Outputs:
- section_out: bfloat16 [32, 256, 2048], P('section', 'tensor')
- grad_magnitude: float32 [32, 2048], P('section')
- grad_a: float32 [32, 8, 14336], P('section', None, 'tensor')
- grad_b: float32 [32, 16, 2048], P('section')
- hidden_grad: bfloat16 [32, 128, 14336], P('section', None, 'tensor')
Inputs may be any that keep to these rules, and one draw needn't show every extreme that they name: frozen projection weights.
All inputs are finite; a program needn't handle non-finite values.
Results may differ from a plain program's by a relative error of at most 0.0057.
Values may be sent and summed in bfloat16 or wider, within the bound.
A program may use at most 64 MiB of HBM per device.

v0:
```python
import jax
import jax.numpy as jnp
from jax import lax
from jax.sharding import PartitionSpec as P

epsilon = 1e-06


def swapped(array, axis, apart):
    return lax.ppermute(array, axis, [(i, i ^ 1 << apart) for i in range(lax.axis_size(axis))])


def from_behind(array, axis, by):
    count = lax.axis_size(axis)
    pairs = [(i, i + by) for i in range(count) if 0 <= i + by < count]
    return lax.ppermute(array, axis, pairs)


def column_norms(squares):
    return jnp.sqrt(lax.psum(squares, "tensor") + epsilon)


def forward_rows(term_fn, own_rows):
    return lax.psum_scatter(
        term_fn(jnp.int32(0), own_rows * lax.axis_size("tensor")),
        "tensor",
        scatter_dimension=0,
        tiled=True,
    )


def local(
    frozen,
    adapter_a,
    adapter_b,
    magnitude,
    hidden_fwd,
    carried,
    embedded,
    hidden_bwd,
    returned,
    head_grad,
):
    base_w = frozen[0]
    fac_half = adapter_a[0]
    fac_b = adapter_b[0]
    mag = magnitude[0]
    own_rows = carried.shape[1]
    slot_id = lax.axis_index("section")
    slot_count = lax.axis_size("section")
    half = slot_id % 2
    first_half = half == 0
    fwd_other, bwd_other, fac_other = swapped(
        (hidden_fwd[0], hidden_bwd[0], fac_half), "section", 0
    )

    def in_order(own, other):
        return jnp.concatenate(
            [jnp.where(first_half, own, other), jnp.where(first_half, other, own)], axis=0
        )

    hid_fwd = in_order(hidden_fwd[0], fwd_other)
    hid_bwd = in_order(hidden_bwd[0], bwd_other)
    fac_a = in_order(fac_half, fac_other)
    width = base_w.shape[1]
    arriving = from_behind(carried[0], "section", 2)
    embed_cols = lax.dynamic_slice_in_dim(embedded, half * width, width, 1)
    inflow = jnp.where(slot_id < 2, embed_cols, arriving)
    coming = from_behind(returned[0], "section", -2)
    head_cols = lax.dynamic_slice_in_dim(head_grad, half * width, width, 1)
    cotangent = jnp.where(slot_id >= slot_count - 2, head_cols, coming)
    merged = (
        base_w.astype(jnp.float32)
        + jnp.einsum("rf,rd->fd", fac_a, fac_b, preferred_element_type=jnp.float32)
    ).astype(jnp.bfloat16)
    merged_f = merged.astype(jnp.float32)
    squares = jnp.sum(merged_f * merged_f, axis=0)
    low_part = jnp.einsum("tf,rf->tr", hid_bwd, fac_a, preferred_element_type=jnp.float32)
    low = lax.psum(low_part, "tensor").astype(jnp.bfloat16)
    col_norms = column_norms(squares)
    col_scale = mag / col_norms

    def scaled_term(offset, amount):
        return jnp.dot(hid_fwd, merged, preferred_element_type=jnp.float32) * col_scale

    projected = forward_rows(scaled_term, own_rows)
    section_out = (inflow.astype(jnp.float32) + projected).astype(jnp.bfloat16)
    all_rows = hid_bwd.shape[0]
    mag_acc = jnp.zeros((width,), jnp.float32)
    scaled_cot = (
        lax.all_gather(cotangent, "tensor", axis=0, tiled=True).astype(jnp.float32) * col_scale
    ).astype(jnp.bfloat16)
    hid_part = jnp.einsum("td,fd->tf", scaled_cot, merged, preferred_element_type=jnp.float32)
    hid_acc = hid_part
    adapt_part = jnp.einsum("td,rd->tr", scaled_cot, fac_b, preferred_element_type=jnp.float32)
    adapt_acc = adapt_part
    grad_b_acc = jnp.einsum("tr,td->rd", low, scaled_cot, preferred_element_type=jnp.float32)
    hid_acc, adapt_acc, grad_b_acc, mag_acc = (hid_acc, adapt_acc, grad_b_acc, mag_acc)
    half_rows = all_rows // 2
    send_hid = lax.dynamic_slice_in_dim(hid_acc, (1 - half) * half_rows, half_rows, 0)
    got_hid, got_adapt = swapped((send_hid, adapt_acc), "section", 0)
    own_hid = lax.dynamic_slice_in_dim(hid_acc, half * half_rows, half_rows, 0)
    hidden_grad = (own_hid + got_hid).astype(jnp.bfloat16)
    adapter_cot = (adapt_acc + got_adapt).astype(jnp.bfloat16)
    rank_half = fac_half.shape[0]
    own_cot = lax.dynamic_slice_in_dim(adapter_cot, half * rank_half, rank_half, 1)
    grad_a = jnp.einsum("tr,tf->rf", own_cot, hid_bwd, preferred_element_type=jnp.float32)
    own_recomputed = lax.psum_scatter(
        jnp.dot(hid_bwd, merged, preferred_element_type=jnp.float32),
        "tensor",
        scatter_dimension=0,
        tiled=True,
    )
    mag_part = jnp.sum(cotangent.astype(jnp.float32) * own_recomputed, axis=0)
    grad_mag = lax.psum(mag_part, "tensor") / col_norms
    return (section_out[None], grad_mag[None], grad_a[None], grad_b_acc[None], hidden_grad[None])


def solution(mesh):
    placed = (
        P("section", "tensor", None),
        P("section", None, "tensor"),
        P("section", None, None),
        P("section", None),
        P("section", None, "tensor"),
        P("section", "tensor", None),
        P("tensor", None),
        P("section", None, "tensor"),
        P("section", "tensor", None),
        P("tensor", None),
    )
    return jax.shard_map(
        local,
        mesh=mesh,
        in_specs=placed,
        out_specs=(
            P("section", "tensor", None),
            P("section", None),
            P("section", None, "tensor"),
            P("section", None, None),
            P("section", None, "tensor"),
        ),
        check_vma=False,
    )
```

profile of v0, /device:TPU:2, one launch (start us, length us, event | category | flops | bytes accessed | tf_op | source)
XLA Modules:
  0.0 222.4 jit_solution(7242099458020499546)
XLA Ops:
  7.2 3.5 %collective-permute-start.2 = (bf16[8,896]{1,0:T(8,128)(2,1)}, bf16[8,896]{1,0:T(8,128)(2,1)S(1)}, u32[]{:S(2)}, u32[]{:S(2)}) collective-permute-start(bf16[8,896]{1,0:T(8,128)(2,1)} %bitcast.37), channel_id=1, source_target_pairs={{0,16},{16,0},{32,48},{48,32},{64,80},{80,64},{96,112},{112,96},{1... | collective-permute-start | bytes 43016 | tf_op jit(solution)/shard_map/ppermute | solution.py:10
  10.7 2.4 %collective-permute-start.4 = (bf16[128,896]{1,0:T(8,128)(2,1)}, bf16[128,896]{1,0:T(8,128)(2,1)S(1)}, u32[]{:S(2)}, u32[]{:S(2)}) collective-permute-start(bf16[128,896]{1,0:T(8,128)(2,1)} %bitcast.35), channel_id=1, source_target_pairs={{0,16},{16,0},{32,48},{48,32},{64,80},{80,64},{96,112},{112,96},{1... | collective-permute-start | bytes 688136 | tf_op jit(solution)/shard_map/ppermute | solution.py:10
  13.8 3.4 %multiply_reduce_fusion = (f32[2048]{0:T(1024)S(1)}, bf16[896,2048]{1,0:T(8,128)(2,1)S(1)}) fusion(bf16[1,16,2048]{2,1,0:T(8,128)(2,1)S(1)} %copy-done, bf16[8,896]{1,0:T(8,128)(2,1)S(1)} %get-tuple-element.15, bf16[8,896]{1,0:T(8,128)(2,1)S(1)} %get-tuple-element.14, bf16[1,896,2048]{2,1,0:T(8,128)(2,1)} %param.10), kind=kOutput, calls=%fused_computation.2 | convolution fusion | flops 69785600 | bytes 7442432 | tf_op jit(solution)/shard_map/rf,rd->fd/dot_general | solution.py:74
  17.2 2.7 %collective-permute-done.4 = bf16[128,896]{1,0:T(8,128)(2,1)S(1)} collective-permute-done((bf16[128,896]{1,0:T(8,128)(2,1)}, bf16[128,896]{1,0:T(8,128)(2,1)S(1)}, u32[]{:S(2)}, u32[]{:S(2)}) %collective-permute-start.4) | collective-permute-done | bytes 229408 | tf_op jit(solution)/shard_map/ppermute | solution.py:10
  20.0 2.6 %fusion.8 = f32[256,2048]{1,0:T(8,128)} fusion(bf16[896,2048]{1,0:T(8,128)(2,1)S(1)} %get-tuple-element.19, bf16[128,896]{1,0:T(8,128)(2,1)S(1)} %get-tuple-element.13, bf16[128,896]{1,0:T(8,128)(2,1)S(1)} %get-tuple-element.12), kind=kOutput, calls=%fused_computation.20 | convolution fusion | flops 940441600 | bytes 6225920 | tf_op jit(solution)/shard_map/dot_general | solution.py:109
  22.7 5.2 %collective-permute-start.3 = (bf16[16,2048]{1,0:T(8,128)(2,1)S(1)}, bf16[16,2048]{1,0:T(8,128)(2,1)S(1)}, u32[]{:S(2)}, u32[]{:S(2)}) collective-permute-start(bf16[16,2048]{1,0:T(8,128)(2,1)S(1)} %bitcast.40), channel_id=1, source_target_pairs={{32,0},{48,16},{64,32},{80,48},{96,64},{112,80},{128,96},{144,112}... | collective-permute-start | bytes 196616 | tf_op jit(solution)/shard_map/ppermute | solution.py:16
  28.0 2.5 %collective-permute-done.3 = bf16[16,2048]{1,0:T(8,128)(2,1)S(1)} collective-permute-done((bf16[16,2048]{1,0:T(8,128)(2,1)S(1)}, bf16[16,2048]{1,0:T(8,128)(2,1)S(1)}, u32[]{:S(2)}, u32[]{:S(2)}) %collective-permute-start.3) | collective-permute-done | bytes 65568 | tf_op jit(solution)/shard_map/ppermute | solution.py:16
  30.5 58.6 %reduce-scatter.5.cloned.1.call-done = f32[16,2048]{1,0:T(8,128)} async-done(((f32[256,2048]{1,0:T(8,128)}), f32[16,2048]{1,0:T(8,128)}) %reduce-scatter.5.cloned.1.call-update) | async-done | bytes 131088 | tf_op jit(solution)/shard_map/reduce_scatter | solution.py:108
  89.1 1.6 multiply_reduce_fusion.1
  90.8 3.6 %collective-permute-start.1 = (bf16[128,896]{1,0:T(8,128)(2,1)S(1)}, bf16[128,896]{1,0:T(8,128)(2,1)S(1)}, u32[]{:S(2)}, u32[]{:S(2)}) collective-permute-start(bf16[128,896]{1,0:T(8,128)(2,1)S(1)} %bitcast.36), channel_id=1, source_target_pairs={{0,16},{16,0},{32,48},{48,32},{64,80},{80,64},{96,112},{112,96},{1... | collective-permute-start | bytes 688136 | tf_op jit(solution)/shard_map/ppermute | solution.py:10
  94.6 4.1 %collective-permute-done.1 = bf16[128,896]{1,0:T(8,128)(2,1)S(1)} collective-permute-done((bf16[128,896]{1,0:T(8,128)(2,1)S(1)}, bf16[128,896]{1,0:T(8,128)(2,1)S(1)}, u32[]{:S(2)}, u32[]{:S(2)}) %collective-permute-start.1) | collective-permute-done | bytes 229408 | tf_op jit(solution)/shard_map/ppermute | solution.py:10
  98.7 50.0 %all-reduce = (f32[2048]{0:T(1024)S(1)}, f32[2048]{0:T(1024)S(1)}, bf16[256,16]{1,0:T(8,128)(2,1)S(1)}) all-reduce(f32[2048]{0:T(1024)S(1)} %get-tuple-element.18, f32[2048]{0:T(1024)S(1)} %get-tuple-element.8, f32[256,16]{1,0:T(8,128)S(1)} %fusion.7), channel_id=1, replica_groups=mesh['section'=32,'tensor'=16] {'tensor'}, use_global_device_ids=true, to_apply=%region_1.2 | all-reduce | flops 8192 | bytes 57344 | tf_op jit(solution)/shard_map/psum | solution.py:20
  149.4 4.6 %convolution_multiply_fusion = f32[256,2048]{1,0:T(8,128)} fusion(bf16[896,2048]{1,0:T(8,128)(2,1)} %copy-done.1, f32[2048]{0:T(1024)S(1)} %get-tuple-element.17, bf16[128,896]{1,0:T(8,128)(2,1)S(1)} %get-tuple-element.11, bf16[128,896]{1,0:T(8,128)(2,1)S(1)} %get-tuple-element.10), kind=kOutput, calls=%fused_computation.3 | convolution fusion | flops 940965888 | bytes 6234112 | tf_op jit(solution)/shard_map/dot_general | solution.py:84
  154.1 3.7 %fusion.1 = f32[256,896]{1,0:T(8,128)S(1)} fusion(bf16[896,2048]{1,0:T(8,128)(2,1)} %copy-done.1, bf16[256,2048]{1,0:T(8,128)(2,1)} %all-gather.2.cloned.1.call-done, f32[2048]{0:T(1024)S(1)} %get-tuple-element.17), kind=kOutput, calls=%fused_computation.7 | convolution fusion | flops 941096960 | bytes 5644288 | tf_op jit(solution)/shard_map/td,fd->tf/dot_general | solution.py:93
  157.9 3.4 %collective-permute-start.6 = (f32[128,896]{1,0:T(8,128)S(1)}, f32[128,896]{1,0:T(8,128)S(1)}, u32[]{:S(2)}, u32[]{:S(2)}) collective-permute-start(f32[128,896]{1,0:T(8,128)S(1)} %constant_dynamic-slice_fusion), channel_id=1, source_target_pairs={{0,16},{16,0},{32,48},{48,32},{64,80},{80,64},{96,112},{112,96},{1... | collective-permute-start | bytes 1376264 | tf_op jit(solution)/shard_map/ppermute | solution.py:10
  161.2 4.3 %collective-permute-start = (bf16[16,2048]{1,0:T(8,128)(2,1)}, bf16[16,2048]{1,0:T(8,128)(2,1)S(1)}, u32[]{:S(2)}, u32[]{:S(2)}) collective-permute-start(bf16[16,2048]{1,0:T(8,128)(2,1)} %bitcast), channel_id=1, source_target_pairs={{0,32},{16,48},{32,64},{48,80},{64,96},{80,112},{96,128},{112,144}... | collective-permute-start | bytes 196616 | tf_op jit(solution)/shard_map/ppermute | solution.py:16
  166.0 2.5 %collective-permute-start.5 = (f32[256,16]{0,1:T(8,128)S(1)}, f32[256,16]{0,1:T(8,128)S(1)}, u32[]{:S(2)}, u32[]{:S(2)}) collective-permute-start(f32[256,16]{0,1:T(8,128)S(1)} %fusion.2), channel_id=1, source_target_pairs={{0,16},{16,0},{32,48},{48,32},{64,80},{80,64},{96,112},{112,96},{1... | collective-permute-start | bytes 49160 | tf_op jit(solution)/shard_map/ppermute | solution.py:10
  168.4 1.0 convolution_bitcast_fusion
  169.4 2.2 collective-permute-done.5
  171.6 0.8 convolution_bitcast_fusion.1
  172.4 0.7 fusion.6
  173.1 1.3 collective-permute-done
  174.5 39.8 %reduce-scatter.3.cloned.1.call-done = f32[16,2048]{1,0:T(8,128)} async-done(((f32[256,2048]{1,0:T(8,128)}), f32[16,2048]{1,0:T(8,128)}) %reduce-scatter.3.cloned.1.call-update) | async-done | bytes 131088 | tf_op jit(solution)/shard_map/reduce_scatter | solution.py:24
  214.3 1.6 fusion.9
  (32 shorter events, 2.4 us)
Async XLA Ops:
  7.2 6.7 %copy-start = (bf16[1,16,2048]{2,1,0:T(8,128)(2,1)S(1)}, bf16[1,16,2048]{2,1,0:T(8,128)(2,1)}, u32[]{:S(2)}) copy-start(bf16[1,16,2048]{2,1,0:T(8,128)(2,1)} %param.12) | copy-start | bytes 196612
  7.2 81.9 %reduce-scatter.5.cloned.1.call-start = ((), (), s32[]{:S(2)}) async-start(), calls=%async_computation.3 | async-start | bytes 2228224 | tf_op jit(solution)/shard_map/reduce_scatter | solution.py:108
  7.2 5.9 %collective-permute-start.2 = (bf16[8,896]{1,0:T(8,128)(2,1)}, bf16[8,896]{1,0:T(8,128)(2,1)S(1)}, u32[]{:S(2)}, u32[]{:S(2)}) collective-permute-start(bf16[8,896]{1,0:T(8,128)(2,1)} %bitcast.37), channel_id=1, source_target_pairs={{0,16},{16,0},{32,48},{48,32},{64,80},{80,64},{96,112},{112,96},{1... | collective-permute-start | bytes 43016 | tf_op jit(solution)/shard_map/ppermute | solution.py:10
  10.7 9.2 %collective-permute-start.4 = (bf16[128,896]{1,0:T(8,128)(2,1)}, bf16[128,896]{1,0:T(8,128)(2,1)S(1)}, u32[]{:S(2)}, u32[]{:S(2)}) collective-permute-start(bf16[128,896]{1,0:T(8,128)(2,1)} %bitcast.35), channel_id=1, source_target_pairs={{0,16},{16,0},{32,48},{48,32},{64,80},{80,64},{96,112},{112,96},{1... | collective-permute-start | bytes 688136 | tf_op jit(solution)/shard_map/ppermute | solution.py:10
  13.8 6.1 %copy-start.3 = (bf16[1,128,896]{2,1,0:T(8,128)(2,1)S(1)}, bf16[1,128,896]{2,1,0:T(8,128)(2,1)}, u32[]{:S(2)}) copy-start(bf16[1,128,896]{2,1,0:T(8,128)(2,1)} %param.17) | copy-start | bytes 688132
  17.2 2.7 %copy-start.1 = (bf16[896,2048]{1,0:T(8,128)(2,1)}, bf16[896,2048]{1,0:T(8,128)(2,1)S(1)}, u32[]{:S(2)}) copy-start(bf16[896,2048]{1,0:T(8,128)(2,1)S(1)} %get-tuple-element.19) | copy-start | bytes 11010052
  20.0 2.8 %copy-start.7 = (bf16[1,16,2048]{2,1,0:T(8,128)(2,1)S(1)}, bf16[1,16,2048]{2,1,0:T(8,128)(2,1)}, u32[]{:S(2)}) copy-start(bf16[1,16,2048]{2,1,0:T(8,128)(2,1)} %param.18) | copy-start | bytes 196612
  20.0 69.1 %copy-start.5 = (bf16[16,4096]{1,0:T(8,128)(2,1)S(1)}, bf16[16,4096]{1,0:T(8,128)(2,1)}, u32[]{:S(2)}) copy-start(bf16[16,4096]{1,0:T(8,128)(2,1)} %param.19) | copy-start | bytes 393220
  20.0 70.8 %copy-start.4 = (bf16[1,128,896]{2,1,0:T(8,128)(2,1)S(1)}, bf16[1,128,896]{2,1,0:T(8,128)(2,1)}, u32[]{:S(2)}) copy-start(bf16[1,128,896]{2,1,0:T(8,128)(2,1)} %param.14) | copy-start | bytes 688132
  22.6 126.1 %copy-start.6 = (f32[1,2048]{1,0:T(1,128)S(1)}, f32[1,2048]{1,0:T(1,128)}, u32[]{:S(2)}) copy-start(f32[1,2048]{1,0:T(1,128)} %param.13) | copy-start | bytes 24580
  22.7 131.4 %all-gather.2.cloned.1.call-start = ((), (), s32[]{:S(2)}) async-start(), calls=%async_computation.4 | async-start | bytes 1114112 | tf_op jit(solution)/shard_map/all_gather | solution.py:91
  22.7 7.8 %collective-permute-start.3 = (bf16[16,2048]{1,0:T(8,128)(2,1)S(1)}, bf16[16,2048]{1,0:T(8,128)(2,1)S(1)}, u32[]{:S(2)}, u32[]{:S(2)}) collective-permute-start(bf16[16,2048]{1,0:T(8,128)(2,1)S(1)} %bitcast.40), channel_id=1, source_target_pairs={{32,0},{48,16},{64,32},{80,48},{96,64},{112,80},{128,96},{144,112}... | collective-permute-start | bytes 196616 | tf_op jit(solution)/shard_map/ppermute | solution.py:16
  90.7 123.6 %reduce-scatter.3.cloned.1.call-start = ((), (), s32[]{:S(2)}) async-start(), calls=%async_computation.2 | async-start | bytes 2228224 | tf_op jit(solution)/shard_map/reduce_scatter | solution.py:24
  90.8 7.9 %collective-permute-start.1 = (bf16[128,896]{1,0:T(8,128)(2,1)S(1)}, bf16[128,896]{1,0:T(8,128)(2,1)S(1)}, u32[]{:S(2)}, u32[]{:S(2)}) collective-permute-start(bf16[128,896]{1,0:T(8,128)(2,1)S(1)} %bitcast.36), channel_id=1, source_target_pairs={{0,16},{16,0},{32,48},{48,32},{64,80},{80,64},{96,112},{112,96},{1... | collective-permute-start | bytes 688136 | tf_op jit(solution)/shard_map/ppermute | solution.py:10
  154.1 11.5 %copy-start.2 = (bf16[256,2048]{1,0:T(8,128)(2,1)S(1)}, bf16[256,2048]{1,0:T(8,128)(2,1)}, u32[]{:S(2)}) copy-start(bf16[256,2048]{1,0:T(8,128)(2,1)} %all-gather.2.cloned.1.call-done) | copy-start | bytes 3145732
  157.9 14.5 %collective-permute-start.6 = (f32[128,896]{1,0:T(8,128)S(1)}, f32[128,896]{1,0:T(8,128)S(1)}, u32[]{:S(2)}, u32[]{:S(2)}) collective-permute-start(f32[128,896]{1,0:T(8,128)S(1)} %constant_dynamic-slice_fusion), channel_id=1, source_target_pairs={{0,16},{16,0},{32,48},{48,32},{64,80},{80,64},{96,112},{112,96},{1... | collective-permute-start | bytes 1376264 | tf_op jit(solution)/shard_map/ppermute | solution.py:10
  161.2 13.2 %collective-permute-start = (bf16[16,2048]{1,0:T(8,128)(2,1)}, bf16[16,2048]{1,0:T(8,128)(2,1)S(1)}, u32[]{:S(2)}, u32[]{:S(2)}) collective-permute-start(bf16[16,2048]{1,0:T(8,128)(2,1)} %bitcast), channel_id=1, source_target_pairs={{0,32},{16,48},{32,64},{48,80},{64,96},{80,112},{96,128},{112,144}... | collective-permute-start | bytes 196616 | tf_op jit(solution)/shard_map/ppermute | solution.py:16
  166.0 5.6 %collective-permute-start.5 = (f32[256,16]{0,1:T(8,128)S(1)}, f32[256,16]{0,1:T(8,128)S(1)}, u32[]{:S(2)}, u32[]{:S(2)}) collective-permute-start(f32[256,16]{0,1:T(8,128)S(1)} %fusion.2), channel_id=1, source_target_pairs={{0,16},{16,0},{32,48},{48,32},{64,80},{80,64},{96,112},{112,96},{1... | collective-permute-start | bytes 49160 | tf_op jit(solution)/shard_map/ppermute | solution.py:10
Sparse Core Ops, SparseCore 0:
  22.8 66.2 reduce-scatter.4
  91.8 40.0 all-gather.1
  154.2 60.0 reduce-scatter.2
where the time goes:
time: 223 us; the launch traced here: 222 us
  waiting for transfers between devices  111 us (50%)
  blocking collectives  50 us (22%)
  starting transfers between devices  24.9 us (11%)
  matrix products  16.7 us (7%)
  between operations  14 us (6%)
  other arithmetic  5.3 us (2%)
    reduce_scatter x1, waiting for transfers between devices, local(): lax.psum_scatter(jnp.dot(hid_bwd, merged, preferred_element_type=jnp.floa...  58.6 us
    psum x1, blocking collectives, column_norms(): return jnp.sqrt(lax.psum(squares, 'tensor') + epsilon)  50 us
    reduce_scatter x1, waiting for transfers between devices, forward_rows(): lax.psum_scatter(term_fn(jnp.int32(0), own_rows * lax.axis_size('tensor')...  39.8 us
    ppermute x5, starting transfers between devices, swapped(): lax.ppermute(array, axis, [(i, i ^ 1 << apart) for i in range(lax.axis_si...  15.2 us
    ppermute x2, starting transfers between devices, from_behind(): return lax.ppermute(array, axis, pairs)  9.55 us
    ppermute x5, waiting for transfers between devices, swapped(): lax.ppermute(array, axis, [(i, i ^ 1 << apart) for i in range(lax.axis_si...  8.95 us
    dot_general x1, matrix products, scaled_term(): jnp.dot(hid_fwd, merged, preferred_element_type=jnp.float32) * col_scale  4.63 us
  transfers between devices with their start and end apart: 10, of which 7 were waited for; matrix products, arithmetic and copies ran while one was open for 7% of the time, Pallas kernels for 0%

commit v1 on v0

--- a/solution.py
+++ b/solution.py
@@ -17,7 +17,7 @@
 
 
 def column_norms(squares):
-    return jnp.sqrt(lax.psum(squares, "tensor") + epsilon)
+    return jnp.sqrt(jnp.sum(lax.all_gather(squares, axis_name="tensor"), axis=0) + epsilon)
 
 
 def forward_rows(term_fn, own_rows):

time: 223 us -> 233 us (1.045)
  the two profiles are of different devices: /device:TPU:2 before, /device:TPU:6 now
where the time goes in v1:
time: 233 us
  waiting for transfers between devices  110 us (47%)
  blocking collectives  62.8 us (27%)
  starting transfers between devices  24.4 us (10%)
  matrix products  16.7 us (7%)
  between operations  14 us (6%)
  other arithmetic  5.31 us (2%)
    reduce_scatter x1, waiting for transfers between devices, local(): lax.psum_scatter(jnp.dot(hid_bwd, merged, preferred_element_type=jnp.floa...  58.9 us
    psum x1, blocking collectives, local(): grad_mag = lax.psum(mag_part, 'tensor') / col_norms  48.2 us
    reduce_scatter x1, waiting for transfers between devices, forward_rows(): lax.psum_scatter(term_fn(jnp.int32(0), own_rows * lax.axis_size('tensor')...  40.1 us
    ppermute x5, starting transfers between devices, swapped(): lax.ppermute(array, axis, [(i, i ^ 1 << apart) for i in range(lax.axis_si...  15.2 us
    all_gather x1, blocking collectives, column_norms(): lax.all_gather(squares, axis_name='tensor')  14.5 us
    ppermute x2, starting transfers between devices, from_behind(): return lax.ppermute(array, axis, pairs)  9.15 us
    ppermute x5, waiting for transfers between devices, swapped(): lax.ppermute(array, axis, [(i, i ^ 1 << apart) for i in range(lax.axis_si...  6.3 us
  transfers between devices with their start and end apart: 10, of which 7 were waited for; matrix products, arithmetic and copies ran while one was open for 7% of the time, Pallas kernels for 0%

profile of v1, /device:TPU:6, one launch (start us, length us, event | category | flops | bytes accessed | tf_op | source)
XLA Modules:
  0.0 233.0 jit_solution(5687648987393418745)
XLA Ops:
  7.2 3.5 %collective-permute-start.2 = (bf16[8,896]{1,0:T(8,128)(2,1)}, bf16[8,896]{1,0:T(8,128)(2,1)S(1)}, u32[]{:S(2)}, u32[]{:S(2)}) collective-permute-start(bf16[8,896]{1,0:T(8,128)(2,1)} %bitcast.43), channel_id=1, source_target_pairs={{0,16},{16,0},{32,48},{48,32},{64,80},{80,64},{96,112},{112,96},{1... | collective-permute-start | bytes 43016 | tf_op jit(solution)/shard_map/ppermute | solution.py:10
  10.7 2.4 %collective-permute-start.4 = (bf16[128,896]{1,0:T(8,128)(2,1)}, bf16[128,896]{1,0:T(8,128)(2,1)S(1)}, u32[]{:S(2)}, u32[]{:S(2)}) collective-permute-start(bf16[128,896]{1,0:T(8,128)(2,1)} %bitcast.36), channel_id=1, source_target_pairs={{0,16},{16,0},{32,48},{48,32},{64,80},{80,64},{96,112},{112,96},{1... | collective-permute-start | bytes 688136 | tf_op jit(solution)/shard_map/ppermute | solution.py:10
  13.1 3.5 %collective-permute-start.1 = (bf16[128,896]{1,0:T(8,128)(2,1)}, bf16[128,896]{1,0:T(8,128)(2,1)S(1)}, u32[]{:S(2)}, u32[]{:S(2)}) collective-permute-start(bf16[128,896]{1,0:T(8,128)(2,1)} %bitcast.37), channel_id=1, source_target_pairs={{0,16},{16,0},{32,48},{48,32},{64,80},{80,64},{96,112},{112,96},{1... | collective-permute-start | bytes 688136 | tf_op jit(solution)/shard_map/ppermute | solution.py:10
  17.3 3.4 %multiply_reduce_fusion = (f32[2048]{0:T(1024)S(1)}, bf16[896,2048]{1,0:T(8,128)(2,1)S(1)}) fusion(bf16[1,16,2048]{2,1,0:T(8,128)(2,1)S(1)} %copy-done, bf16[8,896]{1,0:T(8,128)(2,1)S(1)} %get-tuple-element.14, bf16[8,896]{1,0:T(8,128)(2,1)S(1)} %get-tuple-element.13, bf16[1,896,2048]{2,1,0:T(8,128)(2,1)} %param.10), kind=kOutput, calls=%fused_computation.2 | convolution fusion | flops 69785600 | bytes 7442432 | tf_op jit(solution)/shard_map/rf,rd->fd/dot_general | solution.py:74
  21.4 3.5 %collective-permute-done.1 = bf16[128,896]{1,0:T(8,128)(2,1)S(1)} collective-permute-done((bf16[128,896]{1,0:T(8,128)(2,1)}, bf16[128,896]{1,0:T(8,128)(2,1)S(1)}, u32[]{:S(2)}, u32[]{:S(2)}) %collective-permute-start.1) | collective-permute-done | bytes 229408 | tf_op jit(solution)/shard_map/ppermute | solution.py:10
  25.0 2.6 %fusion.8 = f32[256,2048]{1,0:T(8,128)} fusion(bf16[896,2048]{1,0:T(8,128)(2,1)S(1)} %get-tuple-element.18, bf16[128,896]{1,0:T(8,128)(2,1)S(1)} %get-tuple-element.10, bf16[128,896]{1,0:T(8,128)(2,1)S(1)} %get-tuple-element.9), kind=kOutput, calls=%fused_computation.20 | convolution fusion | flops 940441600 | bytes 6225920 | tf_op jit(solution)/shard_map/dot_general | solution.py:109
  27.7 5.5 %collective-permute-start.3 = (bf16[16,2048]{1,0:T(8,128)(2,1)S(1)}, bf16[16,2048]{1,0:T(8,128)(2,1)S(1)}, u32[]{:S(2)}, u32[]{:S(2)}) collective-permute-start(bf16[16,2048]{1,0:T(8,128)(2,1)S(1)} %bitcast.45), channel_id=1, source_target_pairs={{32,0},{48,16},{64,32},{80,48},{96,64},{112,80},{128,96},{144,112}... | collective-permute-start | bytes 196616 | tf_op jit(solution)/shard_map/ppermute | solution.py:16
  33.2 2.1 collective-permute-done.3
  35.3 58.9 %reduce-scatter.5.cloned.1.call-done = f32[16,2048]{1,0:T(8,128)} async-done(((f32[256,2048]{1,0:T(8,128)}), f32[16,2048]{1,0:T(8,128)}) %reduce-scatter.5.cloned.1.call-update) | async-done | bytes 131088 | tf_op jit(solution)/shard_map/reduce_scatter | solution.py:108
  94.2 1.6 multiply_reduce_fusion.1
  95.9 14.5 %all-gather = f32[32768]{0:T(1024)S(1)} all-gather(f32[2048]{0:T(1024)S(1)} %get-tuple-element.17), channel_id=2, replica_groups=mesh['section'=32,'tensor'=16] {'tensor'}, dimensions={0}, use_global_device_ids=true | all-gather | bytes 139264 | tf_op jit(solution)/shard_map/all_gather | solution.py:20
  110.6 48.2 %all-reduce = (f32[2048]{0:T(1024)S(1)}, bf16[256,16]{0,1:T(8,128)(2,1)S(1)}) all-reduce(f32[2048]{0:T(1024)S(1)} %get-tuple-element.7, f32[256,16]{0,1:T(8,128)S(1)} %fusion.7), channel_id=1, replica_groups=mesh['section'=32,'tensor'=16] {'tensor'}, use_global_device_ids=true, to_apply=%region_5.6 | all-reduce | flops 6144 | bytes 40960 | tf_op jit(solution)/shard_map/psum | solution.py:115
  159.5 4.6 %convolution_multiply_fusion = f32[256,2048]{1,0:T(8,128)} fusion(bf16[896,2048]{1,0:T(8,128)(2,1)} %copy-done.1, f32[2048]{0:T(1024)S(1)} %bitcast.38, bf16[128,896]{1,0:T(8,128)(2,1)S(1)} %get-tuple-element.19, bf16[128,896]{1,0:T(8,128)(2,1)S(1)} %get-tuple-element.20), kind=kOutput, calls=%fused_computation.3 | convolution fusion | flops 940965888 | bytes 6234112 | tf_op jit(solution)/shard_map/dot_general | solution.py:84
  164.2 3.7 %fusion.1 = f32[256,896]{1,0:T(8,128)S(1)} fusion(bf16[896,2048]{1,0:T(8,128)(2,1)} %copy-done.1, bf16[256,2048]{1,0:T(8,128)(2,1)} %all-gather.3.cloned.1.call-done, f32[2048]{0:T(1024)S(1)} %bitcast.39), kind=kOutput, calls=%fused_computation.7 | convolution fusion | flops 941096960 | bytes 5644288 | tf_op jit(solution)/shard_map/td,fd->tf/dot_general | solution.py:93
  168.0 3.4 %collective-permute-start.6 = (f32[128,896]{1,0:T(8,128)S(1)}, f32[128,896]{1,0:T(8,128)S(1)}, u32[]{:S(2)}, u32[]{:S(2)}) collective-permute-start(f32[128,896]{1,0:T(8,128)S(1)} %constant_dynamic-slice_fusion), channel_id=1, source_target_pairs={{0,16},{16,0},{32,48},{48,32},{64,80},{80,64},{96,112},{112,96},{1... | collective-permute-start | bytes 1376264 | tf_op jit(solution)/shard_map/ppermute | solution.py:10
  171.4 3.6 %collective-permute-start = (bf16[16,2048]{1,0:T(8,128)(2,1)S(1)}, bf16[16,2048]{1,0:T(8,128)(2,1)S(1)}, u32[]{:S(2)}, u32[]{:S(2)}) collective-permute-start(bf16[16,2048]{1,0:T(8,128)(2,1)S(1)} %bitcast.46), channel_id=1, source_target_pairs={{0,32},{16,48},{32,64},{48,80},{64,96},{80,112},{96,128},{112,144}... | collective-permute-start | bytes 196616 | tf_op jit(solution)/shard_map/ppermute | solution.py:16
  175.4 2.4 %collective-permute-start.5 = (f32[256,16]{0,1:T(8,128)S(1)}, f32[256,16]{0,1:T(8,128)S(1)}, u32[]{:S(2)}, u32[]{:S(2)}) collective-permute-start(f32[256,16]{0,1:T(8,128)S(1)} %fusion.2), channel_id=1, source_target_pairs={{0,16},{16,0},{32,48},{48,32},{64,80},{80,64},{96,112},{112,96},{1... | collective-permute-start | bytes 49160 | tf_op jit(solution)/shard_map/ppermute | solution.py:10
  177.9 0.9 convolution_bitcast_fusion
  178.8 2.2 collective-permute-done.5
  181.1 0.8 convolution_bitcast_fusion.1
  181.9 0.7 fusion.6
  182.6 2.2 collective-permute-done
  184.8 40.1 %reduce-scatter.3.cloned.1.call-done = f32[16,2048]{1,0:T(8,128)} async-done(((f32[256,2048]{1,0:T(8,128)}), f32[16,2048]{1,0:T(8,128)}) %reduce-scatter.3.cloned.1.call-update) | async-done | bytes 131088 | tf_op jit(solution)/shard_map/reduce_scatter | solution.py:24
  224.9 1.6 fusion.9
  (37 shorter events, 3.0 us)
Async XLA Ops:
  7.2 10.2 %copy-start = (bf16[1,16,2048]{2,1,0:T(8,128)(2,1)S(1)}, bf16[1,16,2048]{2,1,0:T(8,128)(2,1)}, u32[]{:S(2)}) copy-start(bf16[1,16,2048]{2,1,0:T(8,128)(2,1)} %param.12) | copy-start | bytes 196612
  7.2 87.1 %reduce-scatter.5.cloned.1.call-start = ((), (), s32[]{:S(2)}) async-start(), calls=%async_computation.3 | async-start | bytes 2228224 | tf_op jit(solution)/shard_map/reduce_scatter | solution.py:108
  7.2 9.4 %collective-permute-start.2 = (bf16[8,896]{1,0:T(8,128)(2,1)}, bf16[8,896]{1,0:T(8,128)(2,1)S(1)}, u32[]{:S(2)}, u32[]{:S(2)}) collective-permute-start(bf16[8,896]{1,0:T(8,128)(2,1)} %bitcast.43), channel_id=1, source_target_pairs={{0,16},{16,0},{32,48},{48,32},{64,80},{80,64},{96,112},{112,96},{1... | collective-permute-start | bytes 43016 | tf_op jit(solution)/shard_map/ppermute | solution.py:10
  10.7 10.6 %collective-permute-start.4 = (bf16[128,896]{1,0:T(8,128)(2,1)}, bf16[128,896]{1,0:T(8,128)(2,1)S(1)}, u32[]{:S(2)}, u32[]{:S(2)}) collective-permute-start(bf16[128,896]{1,0:T(8,128)(2,1)} %bitcast.36), channel_id=1, source_target_pairs={{0,16},{16,0},{32,48},{48,32},{64,80},{80,64},{96,112},{112,96},{1... | collective-permute-start | bytes 688136 | tf_op jit(solution)/shard_map/ppermute | solution.py:10
  13.1 11.7 %collective-permute-start.1 = (bf16[128,896]{1,0:T(8,128)(2,1)}, bf16[128,896]{1,0:T(8,128)(2,1)S(1)}, u32[]{:S(2)}, u32[]{:S(2)}) collective-permute-start(bf16[128,896]{1,0:T(8,128)(2,1)} %bitcast.37), channel_id=1, source_target_pairs={{0,16},{16,0},{32,48},{48,32},{64,80},{80,64},{96,112},{112,96},{1... | collective-permute-start | bytes 688136 | tf_op jit(solution)/shard_map/ppermute | solution.py:10
  17.3 7.5 %copy-start.3 = (bf16[1,128,896]{2,1,0:T(8,128)(2,1)S(1)}, bf16[1,128,896]{2,1,0:T(8,128)(2,1)}, u32[]{:S(2)}) copy-start(bf16[1,128,896]{2,1,0:T(8,128)(2,1)} %param.17) | copy-start | bytes 688132
  17.3 7.5 %copy-start.4 = (bf16[1,128,896]{2,1,0:T(8,128)(2,1)S(1)}, bf16[1,128,896]{2,1,0:T(8,128)(2,1)}, u32[]{:S(2)}) copy-start(bf16[1,128,896]{2,1,0:T(8,128)(2,1)} %param.14) | copy-start | bytes 688132
  20.7 4.2 %copy-start.1 = (bf16[896,2048]{1,0:T(8,128)(2,1)}, bf16[896,2048]{1,0:T(8,128)(2,1)S(1)}, u32[]{:S(2)}) copy-start(bf16[896,2048]{1,0:T(8,128)(2,1)S(1)} %get-tuple-element.18) | copy-start | bytes 11010052
  24.9 2.8 %copy-start.7 = (bf16[1,16,2048]{2,1,0:T(8,128)(2,1)S(1)}, bf16[1,16,2048]{2,1,0:T(8,128)(2,1)}, u32[]{:S(2)}) copy-start(bf16[1,16,2048]{2,1,0:T(8,128)(2,1)} %param.18) | copy-start | bytes 196612
  24.9 69.3 %copy-start.5 = (bf16[16,4096]{1,0:T(8,128)(2,1)S(1)}, bf16[16,4096]{1,0:T(8,128)(2,1)}, u32[]{:S(2)}) copy-start(bf16[16,4096]{1,0:T(8,128)(2,1)} %param.19) | copy-start | bytes 393220
  24.9 134.5 %copy-start.6 = (f32[1,2048]{1,0:T(1,128)S(1)}, f32[1,2048]{1,0:T(1,128)}, u32[]{:S(2)}) copy-start(f32[1,2048]{1,0:T(1,128)} %param.13) | copy-start | bytes 24580
  27.6 136.6 %all-gather.3.cloned.1.call-start = ((), (), s32[]{:S(2)}) async-start(), calls=%async_computation.4 | async-start | bytes 1114112 | tf_op jit(solution)/shard_map/all_gather | solution.py:91
  27.7 7.6 %collective-permute-start.3 = (bf16[16,2048]{1,0:T(8,128)(2,1)S(1)}, bf16[16,2048]{1,0:T(8,128)(2,1)S(1)}, u32[]{:S(2)}, u32[]{:S(2)}) collective-permute-start(bf16[16,2048]{1,0:T(8,128)(2,1)S(1)} %bitcast.45), channel_id=1, source_target_pairs={{32,0},{48,16},{64,32},{80,48},{96,64},{112,80},{128,96},{144,112}... | collective-permute-start | bytes 196616 | tf_op jit(solution)/shard_map/ppermute | solution.py:16
  95.8 129.1 %reduce-scatter.3.cloned.1.call-start = ((), (), s32[]{:S(2)}) async-start(), calls=%async_computation.2 | async-start | bytes 2228224 | tf_op jit(solution)/shard_map/reduce_scatter | solution.py:24
  164.2 7.2 %copy-start.8 = (bf16[1,16,2048]{2,1,0:T(8,128)(2,1)S(1)}, bf16[1,16,2048]{2,1,0:T(8,128)(2,1)}, u32[]{:S(2)}) copy-start(bf16[1,16,2048]{2,1,0:T(8,128)(2,1)} %param.15) | copy-start | bytes 196612
  164.2 10.9 %copy-start.2 = (bf16[256,2048]{1,0:T(8,128)(2,1)S(1)}, bf16[256,2048]{1,0:T(8,128)(2,1)}, u32[]{:S(2)}) copy-start(bf16[256,2048]{1,0:T(8,128)(2,1)} %all-gather.3.cloned.1.call-done) | copy-start | bytes 3145732
  168.0 13.9 %collective-permute-start.6 = (f32[128,896]{1,0:T(8,128)S(1)}, f32[128,896]{1,0:T(8,128)S(1)}, u32[]{:S(2)}, u32[]{:S(2)}) collective-permute-start(f32[128,896]{1,0:T(8,128)S(1)} %constant_dynamic-slice_fusion), channel_id=1, source_target_pairs={{0,16},{16,0},{32,48},{48,32},{64,80},{80,64},{96,112},{112,96},{1... | collective-permute-start | bytes 1376264 | tf_op jit(solution)/shard_map/ppermute | solution.py:10
  171.4 13.4 %collective-permute-start = (bf16[16,2048]{1,0:T(8,128)(2,1)S(1)}, bf16[16,2048]{1,0:T(8,128)(2,1)S(1)}, u32[]{:S(2)}, u32[]{:S(2)}) collective-permute-start(bf16[16,2048]{1,0:T(8,128)(2,1)S(1)} %bitcast.46), channel_id=1, source_target_pairs={{0,32},{16,48},{32,64},{48,80},{64,96},{80,112},{96,128},{112,144}... | collective-permute-start | bytes 196616 | tf_op jit(solution)/shard_map/ppermute | solution.py:16
  175.4 5.6 %collective-permute-start.5 = (f32[256,16]{0,1:T(8,128)S(1)}, f32[256,16]{0,1:T(8,128)S(1)}, u32[]{:S(2)}, u32[]{:S(2)}) collective-permute-start(f32[256,16]{0,1:T(8,128)S(1)} %fusion.2), channel_id=1, source_target_pairs={{0,16},{16,0},{32,48},{48,32},{64,80},{80,64},{96,112},{112,96},{1... | collective-permute-start | bytes 49160 | tf_op jit(solution)/shard_map/ppermute | solution.py:10
Sparse Core Ops, SparseCore 0:
  27.7 66.4 reduce-scatter.4
  96.9 39.5 all-gather.2
  164.3 60.6 reduce-scatter.2
